TPU v7x, 512 devices: a whole 4x8x8 slice. The times are simulated.
512 devices in a mesh: dp: 8 (over z), seq: 64 (over y, x, core).
Axes of the slice: x: 4, y: 8, z: 8, core: 2. Of those that a mesh axis runs over, the one named last changes fastest.
Arguments:
- tokens: bfloat16 [8, 8192, 1280], P('dp', 'seq'), may hold values from -6 to 6
- place: int32 [64, 128], P('seq'), may hold values from 0 to 127, each once within a row
- kernel: float32 [27, 1280], replicated, may hold values from -1.25 to 1.25
- proj_weight: bfloat16 [1280, 3840], P('seq'), may hold values from -0.15625 to 0.15625
- d_projected: bfloat16 [8, 8192, 3840], P('dp', 'seq'), may hold values from -6 to 6
Outputs:
- projected: bfloat16 [8, 8192, 3840], P('dp', 'seq')
- d_tokens: bfloat16 [8, 8192, 1280], P('dp', 'seq')
- d_kernel: float32 [27, 1280], replicated
Inputs may be any that keep to these rules, and one draw needn't show every extreme that they name: Each row of place holds every number 0 to 127 once.
All inputs are finite; a program needn't handle non-finite values.
Results may differ from a plain program's by a relative error of at most 0.005.
Values may be sent and summed in bfloat16 or wider, within the bound.
No kernel may reach another device: no remote copies, remote signals or barrier semaphores. Data moves between devices by JAX's collectives and lax.ppermute only.
A program may use at most 128 MiB of HBM per device.

v0:
```python
import jax
import jax.numpy as jnp
from jax import lax
from jax.sharding import PartitionSpec as P

INLINE = 8
CROSS = 8


def with_halo(value, sides, width):
    for axis, dim in sides:
        size, length = (lax.axis_size(axis), value.shape[dim])
        up = [(i, (i + 1) % size) for i in range(size - 1)]
        down = [(j, i) for i, j in up]
        last = lax.slice_in_dim(value, length - width, length, axis=dim)
        first = lax.slice_in_dim(value, 0, width, axis=dim)
        before = lax.ppermute(last, axis, up)
        after = lax.ppermute(first, axis, down)
        value = jnp.concatenate([before, value, after], axis=dim)
    return value


def brick_cells(landed, inverse):
    tokens_dev = inverse.shape[0]
    width = landed.shape[-1]
    slots = landed.reshape(tokens_dev, width)
    cells = jnp.take(slots, inverse, axis=0)
    return cells.reshape(tokens_dev // (INLINE * CROSS), INLINE, CROSS, width)


def scan_pieces(cells, order, count):
    width = cells.shape[-1]
    tokens_dev = order.shape[0]
    slots = jnp.take(cells.reshape(tokens_dev, width), order, axis=0)
    return slots.reshape(count, tokens_dev // count, width)


def to_bricks(rows, inverse, count):
    tokens_dev, width = rows.shape
    landed = lax.all_to_all(
        rows.reshape(count, tokens_dev // count, width),
        "seq",
        split_axis=0,
        concat_axis=0,
        tiled=True,
    )
    return brick_cells(landed, inverse)


def to_scan(cells, order, count):
    landed = lax.all_to_all(
        scan_pieces(cells, order, count), "seq", split_axis=0, concat_axis=0, tiled=True
    )
    return landed.reshape(order.shape[0], cells.shape[-1])


def with_faces(block):
    deeper = with_halo(block, (("seq", 0),), 1)
    return jnp.pad(deeper, ((0, 0), (1, 1), (1, 1), (0, 0)))


def window(field, depth_dev, start_z, start_i, start_c):
    return field[
        start_z : start_z + depth_dev, start_i : start_i + INLINE, start_c : start_c + CROSS
    ].astype(jnp.float32)


def forward_conv(grid_x, pad_x, kernel, depth_dev):
    conv = jnp.zeros(grid_x.shape, jnp.float32)
    for offset in range(27):
        conv = conv + kernel[offset] * window(
            pad_x, depth_dev, offset // 9, offset // 3 % 3, offset % 3
        )
    return (grid_x.astype(jnp.float32) + conv).astype(jnp.bfloat16)


def backward_conv(grid_d, pad_d, pad_x, kernel, depth_dev):
    grid_float = grid_d.astype(jnp.float32)
    back = grid_float
    partial_value = []
    for offset in range(27):
        dz, di, dc = (offset // 9, offset // 3 % 3, offset % 3)
        back = back + kernel[offset] * window(pad_d, depth_dev, 2 - dz, 2 - di, 2 - dc)
        partial_value.append(
            jnp.sum(grid_float * window(pad_x, depth_dev, dz, di, dc), axis=(0, 1, 2))
        )
    return (back.astype(jnp.bfloat16), jnp.stack(partial_value))


def shards(tokens, place, kernel, proj_weight, d_projected):
    count = lax.axis_size("seq")
    order = place[0]
    inverse = jnp.argsort(order)
    rows_x = tokens[0]
    d_rows = d_projected[0]
    depth_dev = rows_x.shape[0] // (INLINE * CROSS)
    d_y = lax.dot_general(
        d_rows,
        lax.all_gather(proj_weight, "seq", axis=0, tiled=True),
        (((1,), (1,)), ((), ())),
        preferred_element_type=jnp.float32,
    )
    d_y = d_y.astype(jnp.bfloat16)
    grid_x = to_bricks(rows_x, inverse, count)
    pad_x = with_faces(grid_x)
    grid_y = forward_conv(grid_x, pad_x, kernel, depth_dev)
    rows_y = to_scan(grid_y, order, count)
    grid_d = to_bricks(d_y, inverse, count)
    pad_d = with_faces(grid_d)
    back, partial_value = backward_conv(grid_d, pad_d, pad_x, kernel, depth_dev)
    d_tokens = to_scan(back, order, count)
    projected = jnp.dot(
        rows_y,
        lax.all_gather(proj_weight, "seq", axis=0, tiled=True),
        preferred_element_type=jnp.float32,
    )
    projected = projected.astype(jnp.bfloat16)
    d_kernel = lax.psum(partial_value, ("dp", "seq"))
    return (projected[None], d_tokens[None], d_kernel)


def solution(mesh):
    placed = (P("dp", "seq", None), P("seq", None), P(), P("seq", None), P("dp", "seq", None))
    return jax.shard_map(
        shards,
        mesh=mesh,
        in_specs=placed,
        out_specs=(P("dp", "seq", None), P("dp", "seq", None), P()),
        check_vma=False,
    )
```

profile of v0, /device:TPU:1, one launch (start us, length us, event | category | flops | bytes accessed | tf_op | source)
XLA Modules:
  0.0 491.7 jit_solution(6049392206160936502)
XLA Ops:
  7.2 0.7 all-gather.3.cloned.1.call-update
  7.9 1.8 reshape_squeeze.3
  9.7 11.6 %all-to-all-start = ((bf16[64,2,1280]{2,1,0:T(2,128)(2,1)}), bf16[64,2,1280]{2,1,0:T(2,128)(2,1)S(1)}, u32[]{:S(2)}, u32[]{:S(2)}) async-start(bf16[64,2,1280]{2,1,0:T(2,128)(2,1)} %reshape_squeeze.3), calls=%async_computation | async-start | bytes 655360 | tf_op jit(solution)/shard_map/all_to_all | solution.py:40
  21.4 3.2 sort.17
  24.6 1.9 slice_reduce_fusion.25
  26.5 0.7 compare_select_fusion
  27.1 83.8 %all-gather.3.cloned.1.call-done = bf16[64,20,3840]{2,1,0:T(8,128)(2,1)} async-done(((bf16[1,20,3840]{2,1,0:T(8,128)(2,1)}), bf16[64,20,3840]{2,1,0:T(8,128)(2,1)}) %all-gather.3.cloned.1.call-update) | async-done | bytes 9830416 | tf_op jit(solution)/shard_map/all_gather | solution.py:114
  110.9 13.7 %reshape.119 = bf16[1280,3840]{1,0:T(8,128)(2,1)} reshape(bf16[64,20,3840]{2,1,0:T(8,128)(2,1)} %all-gather.3.cloned.1.call-done) | data formatting | bytes 19660800
  124.6 7.1 %convolution_convert_fusion.1 = bf16[128,1280]{1,0:T(8,128)(2,1)S(1)} fusion(bf16[1280,3840]{1,0:T(8,128)(2,1)} %reshape.119, bf16[1,128,3840]{2,1,0:T(8,128)(2,1)S(1)} %copy-done), kind=kOutput, calls=%fused_computation.41 | convolution fusion | flops 1258455040 | bytes 11141120 | tf_op jit(solution)/shard_map/dot_general | solution.py:97
  131.7 0.9 reshape.77
  132.6 5.7 %all-to-all-start.2 = ((bf16[64,2,1280]{2,1,0:T(2,128)(2,1)}), bf16[64,2,1280]{2,1,0:T(2,128)(2,1)S(1)}, u32[]{:S(2)}, u32[]{:S(2)}) async-start(bf16[64,2,1280]{2,1,0:T(2,128)(2,1)} %reshape.77), calls=%async_computation.2 | async-start | bytes 655360 | tf_op jit(solution)/shard_map/all_to_all | solution.py:40
  138.3 0.6 pad_clamp_fusion
  138.8 0.9 slice_reduce_fusion.26
  139.7 0.5 compare_and_fusion
  140.3 0.9 gather_fusion
  141.2 11.2 %all-to-all-done.2 = bf16[64,2,1280]{2,1,0:T(2,128)(2,1)S(1)} async-done(((bf16[64,2,1280]{2,1,0:T(2,128)(2,1)}), bf16[64,2,1280]{2,1,0:T(2,128)(2,1)S(1)}, u32[]{:S(2)}, u32[]{:S(2)}) %all-to-all-start.2) | async-done | bytes 327712 | tf_op jit(solution)/shard_map/all_to_all | solution.py:40
  152.6 0.9 gather_fusion.2
  153.6 0.8 multiply_reduce_fusion
  154.4 2.1 collective-permute-start.1
  156.5 3.5 collective-permute-start
  160.0 0.7 slice_bitcast_fusion.1
  160.7 1.9 collective-permute-start.2
  162.7 3.1 collective-permute-start.3
  165.8 0.6 select_maximum_fusion.2
  166.5 2.5 fusion.83
  169.0 1.7 gather_fusion.1
  170.7 1.5 select_maximum_fusion
  172.2 3.4 add_convert_fusion
  175.7 1.9 gather_fusion.3
  177.5 1.9 broadcast_select_fusion
  179.5 1.8 reshape.75
  181.3 9.7 %all-to-all-start.1 = ((bf16[64,2,1280]{2,1,0:T(2,128)(2,1)}), bf16[64,2,1280]{2,1,0:T(2,128)(2,1)}, u32[]{:S(2)}, u32[]{:S(2)}) async-start(bf16[64,2,1280]{2,1,0:T(2,128)(2,1)} %reshape.75), calls=%async_computation.1 | async-start | bytes 655360 | tf_op jit(solution)/shard_map/all_to_all | solution.py:51
  190.9 0.6 stack.97
  191.5 0.8 reshape.81
  192.4 2.4 fusion.82
  194.8 10.2 %all-to-all-done.1 = bf16[64,2,1280]{2,1,0:T(2,128)(2,1)} async-done(((bf16[64,2,1280]{2,1,0:T(2,128)(2,1)}), bf16[64,2,1280]{2,1,0:T(2,128)(2,1)}, u32[]{:S(2)}, u32[]{:S(2)}) %all-to-all-start.1) | async-done | bytes 327712 | tf_op jit(solution)/shard_map/all_to_all | solution.py:51
  205.0 5.2 %all-to-all-start.3 = ((bf16[64,2,1280]{2,1,0:T(2,128)(2,1)}), bf16[64,2,1280]{2,1,0:T(2,128)(2,1)}, u32[]{:S(2)}, u32[]{:S(2)}) async-start(bf16[64,2,1280]{2,1,0:T(2,128)(2,1)} %reshape.81), calls=%async_computation.3 | async-start | bytes 655360 | tf_op jit(solution)/shard_map/all_to_all | solution.py:51
  210.3 1.5 fusion.78
  211.9 0.7 stack.110
  212.7 0.7 stack.109
  213.4 0.7 stack.108
  214.1 0.7 stack.107
  215.0 3.4 stack.111
  218.4 1.1 reshape.76
  219.5 6.2 %fusion = bf16[1,128,3840]{2,1,0:T(8,128)(2,1)} fusion(bf16[128,1280]{1,0:T(8,128)(2,1)S(1)} %reshape.76, bf16[1280,3840]{1,0:T(8,128)(2,1)} %reshape.119), kind=kOutput, calls=%fused_computation.37 | convolution fusion | flops 1258782720 | bytes 11141120 | tf_op jit(solution)/shard_map/dot_general | solution.py:112
  225.7 1.8 broadcast_in_dim_reshape.3
  227.5 255.8 %all-reduce.4.cloned.1.call-done = f32[27,1280]{1,0:T(8,128)} async-done(((f32[27,1280]{1,0:T(8,128)}), f32[27,1280]{1,0:T(8,128)}) %all-reduce.4.cloned.1.call-update) | async-done | bytes 138256 | tf_op jit(solution)/shard_map/psum | solution.py:118
  483.3 1.6 copy.9
  (78 shorter events, 0.6 us)
Async XLA Ops:
  7.2 117.5 %copy-start = (bf16[1,128,3840]{2,1,0:T(8,128)(2,1)S(1)}, bf16[1,128,3840]{2,1,0:T(8,128)(2,1)}, u32[]{:S(2)}) copy-start(bf16[1,128,3840]{2,1,0:T(8,128)(2,1)} %param.11) | copy-start | bytes 2949124
  7.2 103.8 %all-gather.3.cloned.1.call-start = ((), (), s32[]{:S(2)}) async-start(), calls=%async_computation.5 | async-start | bytes 11980800 | tf_op jit(solution)/shard_map/all_gather | solution.py:114
  9.7 122.8 %all-to-all-start = ((bf16[64,2,1280]{2,1,0:T(2,128)(2,1)}), bf16[64,2,1280]{2,1,0:T(2,128)(2,1)S(1)}, u32[]{:S(2)}, u32[]{:S(2)}) async-start(bf16[64,2,1280]{2,1,0:T(2,128)(2,1)} %reshape_squeeze.3), calls=%async_computation | async-start | bytes 655360 | tf_op jit(solution)/shard_map/all_to_all | solution.py:40
  124.6 14.2 %copy-start.4 = (f32[27,1280]{1,0:T(8,128)S(1)}, f32[27,1280]{1,0:T(8,128)}, u32[]{:S(2)}) copy-start(f32[27,1280]{1,0:T(8,128)} %param.9) | copy-start | bytes 414724
  124.6 15.1 %copy-start.19 = (s32[1,128]{1,0:T(1,128)S(1)}, s32[1,128]{1,0:T(1,128)}, u32[]{:S(2)}) copy-start(s32[1,128]{1,0:T(1,128)} %param.8) | copy-start | bytes 1540
  132.6 19.9 %all-to-all-start.2 = ((bf16[64,2,1280]{2,1,0:T(2,128)(2,1)}), bf16[64,2,1280]{2,1,0:T(2,128)(2,1)S(1)}, u32[]{:S(2)}, u32[]{:S(2)}) async-start(bf16[64,2,1280]{2,1,0:T(2,128)(2,1)} %reshape.77), calls=%async_computation.2 | async-start | bytes 655360 | tf_op jit(solution)/shard_map/all_to_all | solution.py:40
  153.5 12.9 %copy-start.5 = (f32[1280]{0:T(1024)S(1)}, f32[1280]{0:T(1024)}, u32[]{:S(2)}) copy-start(f32[1280]{0:T(1024)} %get-tuple-element.52) | copy-start | bytes 15364
  153.5 12.9 %copy-start.6 = (f32[1280]{0:T(1024)S(1)}, f32[1280]{0:T(1024)}, u32[]{:S(2)}) copy-start(f32[1280]{0:T(1024)} %get-tuple-element.53) | copy-start | bytes 15364
  153.5 12.9 %copy-start.7 = (f32[1280]{0:T(1024)S(1)}, f32[1280]{0:T(1024)}, u32[]{:S(2)}) copy-start(f32[1280]{0:T(1024)} %get-tuple-element.54) | copy-start | bytes 15364
  153.5 12.9 %copy-start.8 = (f32[1280]{0:T(1024)S(1)}, f32[1280]{0:T(1024)}, u32[]{:S(2)}) copy-start(f32[1280]{0:T(1024)} %get-tuple-element.55) | copy-start | bytes 15364
  153.5 12.9 %copy-start.9 = (f32[1280]{0:T(1024)S(1)}, f32[1280]{0:T(1024)}, u32[]{:S(2)}) copy-start(f32[1280]{0:T(1024)} %get-tuple-element.56) | copy-start | bytes 15364
  153.5 12.9 %copy-start.10 = (f32[1280]{0:T(1024)S(1)}, f32[1280]{0:T(1024)}, u32[]{:S(2)}) copy-start(f32[1280]{0:T(1024)} %get-tuple-element.57) | copy-start | bytes 15364
  153.5 12.9 %copy-start.11 = (f32[1280]{0:T(1024)S(1)}, f32[1280]{0:T(1024)}, u32[]{:S(2)}) copy-start(f32[1280]{0:T(1024)} %get-tuple-element.58) | copy-start | bytes 15364
  153.5 12.9 %copy-start.12 = (f32[1280]{0:T(1024)S(1)}, f32[1280]{0:T(1024)}, u32[]{:S(2)}) copy-start(f32[1280]{0:T(1024)} %get-tuple-element.59) | copy-start | bytes 15364
  153.5 12.9 %copy-start.13 = (f32[1280]{0:T(1024)S(1)}, f32[1280]{0:T(1024)}, u32[]{:S(2)}) copy-start(f32[1280]{0:T(1024)} %get-tuple-element.60) | copy-start | bytes 15364
  153.6 12.9 %copy-start.14 = (f32[1280]{0:T(1024)S(1)}, f32[1280]{0:T(1024)}, u32[]{:S(2)}) copy-start(f32[1280]{0:T(1024)} %get-tuple-element.61) | copy-start | bytes 15364
  153.6 12.9 %copy-start.15 = (f32[1280]{0:T(1024)S(1)}, f32[1280]{0:T(1024)}, u32[]{:S(2)}) copy-start(f32[1280]{0:T(1024)} %get-tuple-element.62) | copy-start | bytes 15364
  153.6 12.9 %copy-start.16 = (f32[1280]{0:T(1024)S(1)}, f32[1280]{0:T(1024)}, u32[]{:S(2)}) copy-start(f32[1280]{0:T(1024)} %get-tuple-element.63) | copy-start | bytes 15364
  153.6 12.9 %copy-start.17 = (f32[1280]{0:T(1024)S(1)}, f32[1280]{0:T(1024)}, u32[]{:S(2)}) copy-start(f32[1280]{0:T(1024)} %get-tuple-element.64) | copy-start | bytes 15364
  154.4 14.5 %copy-start.1 = (bf16[128,1280]{1,0:T(8,128)(2,1)}, bf16[128,1280]{1,0:T(8,128)(2,1)S(1)}, u32[]{:S(2)}) copy-start(bf16[128,1280]{1,0:T(8,128)(2,1)S(1)} %get-tuple-element.67) | copy-start | bytes 983044
  154.4 11.3 %collective-permute-start.1 = (bf16[1,8,8,1280]{3,2,1,0:T(8,128)(2,1)S(1)}, bf16[1,8,8,1280]{3,2,1,0:T(8,128)(2,1)S(1)}, u32[]{:S(2)}, u32[]{:S(2)}) collective-permute-start(bf16[1,8,8,1280]{3,2,1,0:T(8,128)(2,1)S(1)} %get-tuple-element.70), channel_id=1, source_target_pairs={{1,0},{2,1},{3,2},{4,3},{5,4},{6,5},{7,6},{8,7},{9,8},{10,9},{11,1... | collective-permute-start | bytes 491528 | tf_op jit(solution)/shard_map/ppermute | solution.py:18
  156.5 9.2 %collective-permute-start = (bf16[1,8,8,1280]{3,2,1,0:T(8,128)(2,1)S(1)}, bf16[1,8,8,1280]{3,2,1,0:T(8,128)(2,1)S(1)}, u32[]{:S(2)}, u32[]{:S(2)}) collective-permute-start(bf16[1,8,8,1280]{3,2,1,0:T(8,128)(2,1)S(1)} %get-tuple-element.71), channel_id=1, source_target_pairs={{0,1},{1,2},{2,3},{3,4},{4,5},{5,6},{6,7},{7,8},{8,9},{9,10},{10,1... | collective-permute-start | bytes 491528 | tf_op jit(solution)/shard_map/ppermute | solution.py:17
  160.7 10.0 %collective-permute-start.2 = (bf16[1,8,8,1280]{3,2,1,0:T(8,128)(2,1)}, bf16[1,8,8,1280]{3,2,1,0:T(8,128)(2,1)}, u32[]{:S(2)}, u32[]{:S(2)}) collective-permute-start(bf16[1,8,8,1280]{3,2,1,0:T(8,128)(2,1)} %get-tuple-element.68), channel_id=1, source_target_pairs={{0,1},{1,2},{2,3},{3,4},{4,5},{5,6},{6,7},{7,8},{8,9},{9,10},{10,1... | collective-permute-start | bytes 491528 | tf_op jit(solution)/shard_map/ppermute | solution.py:17
  162.7 8.0 %collective-permute-start.3 = (bf16[1,8,8,1280]{3,2,1,0:T(8,128)(2,1)}, bf16[1,8,8,1280]{3,2,1,0:T(8,128)(2,1)}, u32[]{:S(2)}, u32[]{:S(2)}) collective-permute-start(bf16[1,8,8,1280]{3,2,1,0:T(8,128)(2,1)} %get-tuple-element.69), channel_id=1, source_target_pairs={{1,0},{2,1},{3,2},{4,3},{5,4},{6,5},{7,6},{8,7},{9,8},{10,9},{11,1... | collective-permute-start | bytes 491528 | tf_op jit(solution)/shard_map/ppermute | solution.py:18
  165.7 3.2 copy-start.3
  175.6 15.3 %copy-start.18 = (f32[1280]{0:T(1024)S(1)}, f32[1280]{0:T(1024)}, u32[]{:S(2)}) copy-start(f32[1280]{0:T(1024)} %get-tuple-element.65) | copy-start | bytes 15364
  181.3 23.8 %all-to-all-start.1 = ((bf16[64,2,1280]{2,1,0:T(2,128)(2,1)}), bf16[64,2,1280]{2,1,0:T(2,128)(2,1)}, u32[]{:S(2)}, u32[]{:S(2)}) async-start(bf16[64,2,1280]{2,1,0:T(2,128)(2,1)} %reshape.75), calls=%async_computation.1 | async-start | bytes 655360 | tf_op jit(solution)/shard_map/all_to_all | solution.py:51
  192.4 18.0 %copy-start.2 = (bf16[128,1280]{1,0:T(8,128)(2,1)S(1)}, bf16[128,1280]{1,0:T(8,128)(2,1)}, u32[]{:S(2)}) copy-start(bf16[128,1280]{1,0:T(8,128)(2,1)} %copy-done.1) | copy-start | bytes 983044
  205.0 20.6 %all-to-all-start.3 = ((bf16[64,2,1280]{2,1,0:T(2,128)(2,1)}), bf16[64,2,1280]{2,1,0:T(2,128)(2,1)}, u32[]{:S(2)}, u32[]{:S(2)}) async-start(bf16[64,2,1280]{2,1,0:T(2,128)(2,1)} %reshape.81), calls=%async_computation.3 | async-start | bytes 655360 | tf_op jit(solution)/shard_map/all_to_all | solution.py:51
  210.3 273.0 %all-reduce.4.cloned.1.call-start = ((), (), s32[]{:S(2)}) async-start(), calls=%async_computation.4 | async-start | bytes 327680 | tf_op jit(solution)/shard_map/psum | solution.py:118
Sparse Core Ops, SparseCore 0:
  11.3 99.6 all-gather.2
  218.5 264.7 all-reduce.3
where the time goes:
time: 493 us; the launch traced here: 492 us
  waiting for transfers between devices  362 us (73%)
  starting transfers between devices  42.8 us (9%)
  local copies, waits for them, and re-layouts  39.6 us (8%)
  other arithmetic  19.6 us (4%)
  between operations  14.6 us (3%)
  matrix products  13.3 us (3%)
    psum x1, waiting for transfers between devices, shards(): d_kernel = lax.psum(partial_value, ('dp', 'seq'))  256 us
    all_gather x1, waiting for transfers between devices, shards(): lax.all_gather(proj_weight, 'seq', axis=0, tiled=True)  83.8 us
    all_to_all x2, starting transfers between devices, to_bricks(): lax.all_to_all(rows.reshape(count, tokens_dev // count, width), 'seq', sp...  17.3 us
    unnamed x42, local copies, waits for them, and re-layouts  15.4 us
    all_to_all x2, starting transfers between devices, to_scan(): lax.all_to_all(scan_pieces(cells, order, count), 'seq', split_axis=0, con...  14.9 us
    all_to_all x2, waiting for transfers between devices, to_bricks(): lax.all_to_all(rows.reshape(count, tokens_dev // count, width), 'seq', sp...  11.2 us
    all_to_all x2, waiting for transfers between devices, to_scan(): lax.all_to_all(scan_pieces(cells, order, count), 'seq', split_axis=0, con...  10.3 us
  transfers between devices with their start and end apart: 10, of which 4 were waited for; matrix products, arithmetic and copies ran while one was open for 12% of the time, Pallas kernels for 0%

commit v1 on v0

--- a/solution.py
+++ b/solution.py
@@ -115,7 +115,7 @@
         preferred_element_type=jnp.float32,
     )
     projected = projected.astype(jnp.bfloat16)
-    d_kernel = lax.psum(partial_value, ("dp", "seq"))
+    d_kernel = lax.psum(lax.psum(partial_value, "dp"), "seq")
     return (projected[None], d_tokens[None], d_kernel)
 
 

time: 493 us -> 473 us (0.959)
  waiting for transfers between devices: 362 us -> 349 us
    psum x1 -> x2, waiting for transfers between devices: 256 us -> 246 us  [shards(): d_kernel = lax.psum(lax.psum(partial_value, 'dp'), 'seq')]
    unnamed x42 -> x44, local copies, waits for them, and re-layouts: 15.4 us -> 15.4 us
  transfers between devices with their start and end apart: 10 -> 11, of which waited for: 4 -> 5; matrix products, arithmetic and copies ran while one was open for 12% -> 11% of each run, Pallas kernels for 0% -> 0%
where the time goes in v1:
time: 473 us; the launch traced here: 472 us
  waiting for transfers between devices  349 us (74%)
  starting transfers between devices  42.7 us (9%)
  local copies, waits for them, and re-layouts  35 us (7%)
  other arithmetic  17.6 us (4%)
  between operations  14.4 us (3%)
  matrix products  13.3 us (3%)
    psum x2, waiting for transfers between devices, shards(): d_kernel = lax.psum(lax.psum(partial_value, 'dp'), 'seq')  246 us
    all_gather x1, waiting for transfers between devices, shards(): lax.all_gather(proj_weight, 'seq', axis=0, tiled=True)  83.9 us
    all_to_all x2, starting transfers between devices, to_bricks(): lax.all_to_all(rows.reshape(count, tokens_dev // count, width), 'seq', sp...  17.3 us
    unnamed x44, local copies, waits for them, and re-layouts  15.4 us
    all_to_all x2, starting transfers between devices, to_scan(): lax.all_to_all(scan_pieces(cells, order, count), 'seq', split_axis=0, con...  14.7 us
    all_to_all x2, waiting for transfers between devices, to_bricks(): lax.all_to_all(rows.reshape(count, tokens_dev // count, width), 'seq', sp...  11.1 us
  transfers between devices with their start and end apart: 11, of which 5 were waited for; matrix products, arithmetic and copies ran while one was open for 11% of the time, Pallas kernels for 0%

profile of v1, /device:TPU:1, one launch (start us, length us, event | category | flops | bytes accessed | tf_op | source)
XLA Modules:
  0.0 471.6 jit_solution(7832719346456000774)
XLA Ops:
  7.2 0.7 all-gather.3.cloned.1.call-update
  7.9 1.8 reshape_squeeze.3
  9.7 11.6 %all-to-all-start = ((bf16[64,2,1280]{2,1,0:T(2,128)(2,1)}), bf16[64,2,1280]{2,1,0:T(2,128)(2,1)S(1)}, u32[]{:S(2)}, u32[]{:S(2)}) async-start(bf16[64,2,1280]{2,1,0:T(2,128)(2,1)} %reshape_squeeze.3), calls=%async_computation | async-start | bytes 655360 | tf_op jit(solution)/shard_map/all_to_all | solution.py:40
  21.4 3.2 sort.17
  24.6 1.8 slice_reduce_fusion.25
  26.4 0.7 compare_select_fusion
  27.0 83.9 %all-gather.3.cloned.1.call-done = bf16[64,20,3840]{2,1,0:T(8,128)(2,1)} async-done(((bf16[1,20,3840]{2,1,0:T(8,128)(2,1)}), bf16[64,20,3840]{2,1,0:T(8,128)(2,1)}) %all-gather.3.cloned.1.call-update) | async-done | bytes 9830416 | tf_op jit(solution)/shard_map/all_gather | solution.py:114
  110.9 13.7 %reshape.119 = bf16[1280,3840]{1,0:T(8,128)(2,1)} reshape(bf16[64,20,3840]{2,1,0:T(8,128)(2,1)} %all-gather.3.cloned.1.call-done) | data formatting | bytes 19660800
  124.6 7.1 %convolution_convert_fusion.1 = bf16[128,1280]{1,0:T(8,128)(2,1)S(1)} fusion(bf16[1280,3840]{1,0:T(8,128)(2,1)} %reshape.119, bf16[1,128,3840]{2,1,0:T(8,128)(2,1)S(1)} %copy-done), kind=kOutput, calls=%fused_computation.41 | convolution fusion | flops 1258455040 | bytes 11141120 | tf_op jit(solution)/shard_map/dot_general | solution.py:97
  131.7 0.9 reshape.77
  132.6 5.7 %all-to-all-start.2 = ((bf16[64,2,1280]{2,1,0:T(2,128)(2,1)}), bf16[64,2,1280]{2,1,0:T(2,128)(2,1)S(1)}, u32[]{:S(2)}, u32[]{:S(2)}) async-start(bf16[64,2,1280]{2,1,0:T(2,128)(2,1)} %reshape.77), calls=%async_computation.2 | async-start | bytes 655360 | tf_op jit(solution)/shard_map/all_to_all | solution.py:40
  138.3 0.6 pad_clamp_fusion
  138.9 0.9 slice_reduce_fusion.26
  139.7 0.6 compare_and_fusion
  140.3 0.1 reshape.72
  140.4 0.9 gather_fusion
  141.3 11.1 %all-to-all-done.2 = bf16[64,2,1280]{2,1,0:T(2,128)(2,1)S(1)} async-done(((bf16[64,2,1280]{2,1,0:T(2,128)(2,1)}), bf16[64,2,1280]{2,1,0:T(2,128)(2,1)S(1)}, u32[]{:S(2)}, u32[]{:S(2)}) %all-to-all-start.2) | async-done | bytes 327712 | tf_op jit(solution)/shard_map/all_to_all | solution.py:40
  152.4 0.1 reshape.78
  152.6 0.9 gather_fusion.2
  153.6 0.2 multiply_reduce_fusion
  153.9 2.1 collective-permute-start.1
  156.0 3.5 collective-permute-start
  159.5 0.7 slice_bitcast_fusion.1
  160.2 0.6 stack.97
  160.8 1.9 collective-permute-start.2
  162.7 3.1 collective-permute-start.3
  165.8 0.6 select_maximum_fusion.2
  166.5 2.5 fusion.83
  169.0 1.7 gather_fusion.1
  170.8 1.5 select_maximum_fusion
  172.3 3.4 add_convert_fusion
  175.7 1.7 gather_fusion.3
  177.4 1.9 broadcast_select_fusion
  179.4 0.8 reshape.75
  180.2 9.7 %all-to-all-start.1 = ((bf16[64,2,1280]{2,1,0:T(2,128)(2,1)}), bf16[64,2,1280]{2,1,0:T(2,128)(2,1)}, u32[]{:S(2)}, u32[]{:S(2)}) async-start(bf16[64,2,1280]{2,1,0:T(2,128)(2,1)} %reshape.75), calls=%async_computation.1 | async-start | bytes 655360 | tf_op jit(solution)/shard_map/all_to_all | solution.py:51
  189.9 1.8 fusion.82
  191.8 0.6 fusion.78
  192.8 2.7 stack.111
  195.5 1.8 reshape.81
  197.3 6.7 %all-to-all-done.1 = bf16[64,2,1280]{2,1,0:T(2,128)(2,1)} async-done(((bf16[64,2,1280]{2,1,0:T(2,128)(2,1)}), bf16[64,2,1280]{2,1,0:T(2,128)(2,1)}, u32[]{:S(2)}, u32[]{:S(2)}) %all-to-all-start.1) | async-done | bytes 327712 | tf_op jit(solution)/shard_map/all_to_all | solution.py:51
  204.0 5.1 %all-to-all-start.3 = ((bf16[64,2,1280]{2,1,0:T(2,128)(2,1)}), bf16[64,2,1280]{2,1,0:T(2,128)(2,1)S(1)}, u32[]{:S(2)}, u32[]{:S(2)}) async-start(bf16[64,2,1280]{2,1,0:T(2,128)(2,1)} %reshape.81), calls=%async_computation.3 | async-start | bytes 655360 | tf_op jit(solution)/shard_map/all_to_all | solution.py:51
  209.1 0.0 all-reduce.7.cloned.1.call-start
  209.1 61.4 %all-reduce.5.cloned.1.call-done = f32[27,1280]{1,0:T(8,128)} async-done(((f32[27,1280]{1,0:T(8,128)}), f32[27,1280]{1,0:T(8,128)}) %all-reduce.5.cloned.1.call-update) | async-done | bytes 138256 | tf_op jit(solution)/shard_map/psum | solution.py:118
  270.6 1.1 reshape.76
  271.7 6.2 %fusion = bf16[1,128,3840]{2,1,0:T(8,128)(2,1)} fusion(bf16[128,1280]{1,0:T(8,128)(2,1)S(1)} %reshape.76, bf16[1280,3840]{1,0:T(8,128)(2,1)} %reshape.119), kind=kOutput, calls=%fused_computation.37 | convolution fusion | flops 1258782720 | bytes 11141120 | tf_op jit(solution)/shard_map/dot_general | solution.py:112
  277.9 0.8 broadcast_in_dim_reshape.3
  278.7 184.8 %all-reduce.7.cloned.1.call-done = f32[27,1280]{1,0:T(8,128)} async-done(((f32[27,1280]{1,0:T(8,128)}), f32[27,1280]{1,0:T(8,128)}) %all-reduce.7.cloned.1.call-update) | async-done | bytes 138256 | tf_op jit(solution)/shard_map/psum | solution.py:118
  463.5 1.6 copy.10
  (83 shorter events, 0.4 us)
Async XLA Ops:
  7.2 117.5 %copy-start = (bf16[1,128,3840]{2,1,0:T(8,128)(2,1)S(1)}, bf16[1,128,3840]{2,1,0:T(8,128)(2,1)}, u32[]{:S(2)}) copy-start(bf16[1,128,3840]{2,1,0:T(8,128)(2,1)} %param.11) | copy-start | bytes 2949124
  7.2 103.8 %all-gather.3.cloned.1.call-start = ((), (), s32[]{:S(2)}) async-start(), calls=%async_computation.6 | async-start | bytes 11980800 | tf_op jit(solution)/shard_map/all_gather | solution.py:114
  9.7 122.8 %all-to-all-start = ((bf16[64,2,1280]{2,1,0:T(2,128)(2,1)}), bf16[64,2,1280]{2,1,0:T(2,128)(2,1)S(1)}, u32[]{:S(2)}, u32[]{:S(2)}) async-start(bf16[64,2,1280]{2,1,0:T(2,128)(2,1)} %reshape_squeeze.3), calls=%async_computation | async-start | bytes 655360 | tf_op jit(solution)/shard_map/all_to_all | solution.py:40
  124.6 14.2 %copy-start.5 = (f32[27,1280]{1,0:T(8,128)S(1)}, f32[27,1280]{1,0:T(8,128)}, u32[]{:S(2)}) copy-start(f32[27,1280]{1,0:T(8,128)} %param.9) | copy-start | bytes 414724
  124.6 15.1 %copy-start.20 = (s32[1,128]{1,0:T(1,128)S(1)}, s32[1,128]{1,0:T(1,128)}, u32[]{:S(2)}) copy-start(s32[1,128]{1,0:T(1,128)} %param.8) | copy-start | bytes 1540
  132.6 19.9 %all-to-all-start.2 = ((bf16[64,2,1280]{2,1,0:T(2,128)(2,1)}), bf16[64,2,1280]{2,1,0:T(2,128)(2,1)S(1)}, u32[]{:S(2)}, u32[]{:S(2)}) async-start(bf16[64,2,1280]{2,1,0:T(2,128)(2,1)} %reshape.77), calls=%async_computation.2 | async-start | bytes 655360 | tf_op jit(solution)/shard_map/all_to_all | solution.py:40
  153.5 12.9 %copy-start.6 = (f32[1280]{0:T(1024)S(1)}, f32[1280]{0:T(1024)}, u32[]{:S(2)}) copy-start(f32[1280]{0:T(1024)} %get-tuple-element.52) | copy-start | bytes 15364
  153.5 12.9 %copy-start.7 = (f32[1280]{0:T(1024)S(1)}, f32[1280]{0:T(1024)}, u32[]{:S(2)}) copy-start(f32[1280]{0:T(1024)} %get-tuple-element.53) | copy-start | bytes 15364
  153.5 12.9 %copy-start.8 = (f32[1280]{0:T(1024)S(1)}, f32[1280]{0:T(1024)}, u32[]{:S(2)}) copy-start(f32[1280]{0:T(1024)} %get-tuple-element.54) | copy-start | bytes 15364
  153.5 12.9 %copy-start.9 = (f32[1280]{0:T(1024)S(1)}, f32[1280]{0:T(1024)}, u32[]{:S(2)}) copy-start(f32[1280]{0:T(1024)} %get-tuple-element.55) | copy-start | bytes 15364
  153.5 12.9 %copy-start.10 = (f32[1280]{0:T(1024)S(1)}, f32[1280]{0:T(1024)}, u32[]{:S(2)}) copy-start(f32[1280]{0:T(1024)} %get-tuple-element.56) | copy-start | bytes 15364
  153.5 12.9 %copy-start.11 = (f32[1280]{0:T(1024)S(1)}, f32[1280]{0:T(1024)}, u32[]{:S(2)}) copy-start(f32[1280]{0:T(1024)} %get-tuple-element.57) | copy-start | bytes 15364
  153.5 12.9 %copy-start.12 = (f32[1280]{0:T(1024)S(1)}, f32[1280]{0:T(1024)}, u32[]{:S(2)}) copy-start(f32[1280]{0:T(1024)} %get-tuple-element.58) | copy-start | bytes 15364
  153.5 12.9 %copy-start.13 = (f32[1280]{0:T(1024)S(1)}, f32[1280]{0:T(1024)}, u32[]{:S(2)}) copy-start(f32[1280]{0:T(1024)} %get-tuple-element.59) | copy-start | bytes 15364
  153.5 12.9 %copy-start.14 = (f32[1280]{0:T(1024)S(1)}, f32[1280]{0:T(1024)}, u32[]{:S(2)}) copy-start(f32[1280]{0:T(1024)} %get-tuple-element.60) | copy-start | bytes 15364
  153.6 12.9 %copy-start.15 = (f32[1280]{0:T(1024)S(1)}, f32[1280]{0:T(1024)}, u32[]{:S(2)}) copy-start(f32[1280]{0:T(1024)} %get-tuple-element.61) | copy-start | bytes 15364
  153.6 12.9 %copy-start.16 = (f32[1280]{0:T(1024)S(1)}, f32[1280]{0:T(1024)}, u32[]{:S(2)}) copy-start(f32[1280]{0:T(1024)} %get-tuple-element.62) | copy-start | bytes 15364
  153.6 12.9 %copy-start.17 = (f32[1280]{0:T(1024)S(1)}, f32[1280]{0:T(1024)}, u32[]{:S(2)}) copy-start(f32[1280]{0:T(1024)} %get-tuple-element.63) | copy-start | bytes 15364
  153.6 12.9 %copy-start.18 = (f32[1280]{0:T(1024)S(1)}, f32[1280]{0:T(1024)}, u32[]{:S(2)}) copy-start(f32[1280]{0:T(1024)} %get-tuple-element.64) | copy-start | bytes 15364
  153.8 15.2 %copy-start.1 = (bf16[128,1280]{1,0:T(8,128)(2,1)}, bf16[128,1280]{1,0:T(8,128)(2,1)S(1)}, u32[]{:S(2)}) copy-start(bf16[128,1280]{1,0:T(8,128)(2,1)S(1)} %get-tuple-element.67) | copy-start | bytes 983044
  153.9 11.9 %collective-permute-start.1 = (bf16[1,8,8,1280]{3,2,1,0:T(8,128)(2,1)S(1)}, bf16[1,8,8,1280]{3,2,1,0:T(8,128)(2,1)S(1)}, u32[]{:S(2)}, u32[]{:S(2)}) collective-permute-start(bf16[1,8,8,1280]{3,2,1,0:T(8,128)(2,1)S(1)} %get-tuple-element.70), channel_id=1, source_target_pairs={{1,0},{2,1},{3,2},{4,3},{5,4},{6,5},{7,6},{8,7},{9,8},{10,9},{11,1... | collective-permute-start | bytes 491528 | tf_op jit(solution)/shard_map/ppermute | solution.py:18
  156.0 9.8 %collective-permute-start = (bf16[1,8,8,1280]{3,2,1,0:T(8,128)(2,1)S(1)}, bf16[1,8,8,1280]{3,2,1,0:T(8,128)(2,1)S(1)}, u32[]{:S(2)}, u32[]{:S(2)}) collective-permute-start(bf16[1,8,8,1280]{3,2,1,0:T(8,128)(2,1)S(1)} %get-tuple-element.71), channel_id=1, source_target_pairs={{0,1},{1,2},{2,3},{3,4},{4,5},{5,6},{6,7},{7,8},{8,9},{9,10},{10,1... | collective-permute-start | bytes 491528 | tf_op jit(solution)/shard_map/ppermute | solution.py:17
  160.8 10.0 %collective-permute-start.2 = (bf16[1,8,8,1280]{3,2,1,0:T(8,128)(2,1)}, bf16[1,8,8,1280]{3,2,1,0:T(8,128)(2,1)}, u32[]{:S(2)}, u32[]{:S(2)}) collective-permute-start(bf16[1,8,8,1280]{3,2,1,0:T(8,128)(2,1)} %get-tuple-element.68), channel_id=1, source_target_pairs={{0,1},{1,2},{2,3},{3,4},{4,5},{5,6},{6,7},{7,8},{8,9},{9,10},{10,1... | collective-permute-start | bytes 491528 | tf_op jit(solution)/shard_map/ppermute | solution.py:17
  162.7 8.0 %collective-permute-start.3 = (bf16[1,8,8,1280]{3,2,1,0:T(8,128)(2,1)}, bf16[1,8,8,1280]{3,2,1,0:T(8,128)(2,1)}, u32[]{:S(2)}, u32[]{:S(2)}) collective-permute-start(bf16[1,8,8,1280]{3,2,1,0:T(8,128)(2,1)} %get-tuple-element.69), channel_id=1, source_target_pairs={{1,0},{2,1},{3,2},{4,3},{5,4},{6,5},{7,6},{8,7},{9,8},{10,9},{11,1... | collective-permute-start | bytes 491528 | tf_op jit(solution)/shard_map/ppermute | solution.py:18
  165.8 3.2 copy-start.3
  180.2 23.8 %all-to-all-start.1 = ((bf16[64,2,1280]{2,1,0:T(2,128)(2,1)}), bf16[64,2,1280]{2,1,0:T(2,128)(2,1)}, u32[]{:S(2)}, u32[]{:S(2)}) async-start(bf16[64,2,1280]{2,1,0:T(2,128)(2,1)} %reshape.75), calls=%async_computation.1 | async-start | bytes 655360 | tf_op jit(solution)/shard_map/all_to_all | solution.py:51
  189.9 1.9 copy-start.2
  189.9 80.7 %all-reduce.5.cloned.1.call-start = ((), (), s32[]{:S(2)}) async-start(), calls=%async_computation.4 | async-start | bytes 327680 | tf_op jit(solution)/shard_map/psum | solution.py:118
  189.9 1.9 copy-start.4
  191.8 1.0 copy-start.19
  204.0 73.9 %all-to-all-start.3 = ((bf16[64,2,1280]{2,1,0:T(2,128)(2,1)}), bf16[64,2,1280]{2,1,0:T(2,128)(2,1)S(1)}, u32[]{:S(2)}, u32[]{:S(2)}) async-start(bf16[64,2,1280]{2,1,0:T(2,128)(2,1)} %reshape.81), calls=%async_computation.3 | async-start | bytes 655360 | tf_op jit(solution)/shard_map/all_to_all | solution.py:51
  209.1 254.4 %all-reduce.7.cloned.1.call-start = ((), (), s32[]{:S(2)}) async-start(), calls=%async_computation.5 | async-start | bytes 327680 | tf_op jit(solution)/shard_map/psum | solution.py:118
Sparse Core Ops, SparseCore 0:
  11.3 99.6 all-gather.2
  195.6 74.8 all-reduce.4
  274.4 189.0 all-reduce.6
